TPU v7x, 32 devices: a whole 2x2x4 slice. The times are simulated.
32 devices in a mesh: param: 2 (over x), row: 4 (over z), col: 4 (over y, core).
Axes of the slice: x: 2, y: 2, z: 4, core: 2. Of those that a mesh axis runs over, the one named last changes fastest.
Arguments:
- coefficients: bfloat16 [3, 2, 32, 512], P(None, None, 'row', 'col'), may hold values from -6 to 6
- noise_sigma: float32 [2, 32, 512], P(None, 'row', 'col'), may hold values from 0.5 to 4
- residual: float32 [2, 32, 512], P(None, 'row', 'col'), may hold values from -0.6 to 0.6
- crack_mask: int32 [32, 4], P('row', 'col'), may hold values 0 or 1
- node_panel: bfloat16 [4, 64, 3, 2048], P('row', 'col', None, 'param'), may hold values from -0.41992188 to 0.41992188
Outputs:
- hessian: float32 [2048, 2048], P('param', ('row', 'col'))
- gradient: float32 [2048], P(('param', 'row', 'col'))
All inputs are finite; a program needn't handle non-finite values. No bound on the sum of `crack_mask` on one device may be relied on, other than what follows from the above.
Results may differ from a plain program's by a relative error of at most 0.0055.
Values may be sent and summed in bfloat16 or wider, within the bound.
A program may use at most 64 MiB of HBM per device.

v0:
```python
import jax
import jax.numpy as jnp
from jax import lax
from jax.sharding import PartitionSpec as P

EL = 8
CAMS = 2


def shifted(block, axis, distance):
    devices = range(lax.axis_size(axis))
    route = [(i - distance, i) for i in devices if i - distance in devices]
    return lax.ppermute(block, axis, route)


def corner_shapes(rows, cols):
    vertical = ((jnp.arange(rows) % EL).astype(jnp.float32) + 0.5) / EL
    horizontal = ((jnp.arange(cols) % EL).astype(jnp.float32) + 0.5) / EL
    lower = vertical[:, None]
    right = horizontal[None, :]
    return jnp.stack(
        [(1.0 - lower) * (1.0 - right), (1.0 - lower) * right, lower * (1.0 - right), lower * right]
    )


def pixel_rows(design, extended):
    corners = jnp.stack(
        [extended[:-1, :-1], extended[:-1, 1:], extended[1:, :-1], extended[1:, 1:]], axis=2
    )
    width = extended.shape[3]
    corners = corners.reshape(design.shape[1], 12, width)
    sensitivity = jnp.einsum("kep,ekq->epq", design, corners, preferred_element_type=jnp.float32)
    return sensitivity.astype(jnp.bfloat16).reshape(design.shape[1] * design.shape[2], width)


def block_product(own_rows, other_rows):
    return lax.dot_general(
        own_rows, other_rows, (((0,), (0,)), ((), ())), preferred_element_type=jnp.float32
    )


def on_device(coefficients, noise_sigma, residual, crack_mask, node_panel):
    rows = noise_sigma.shape[1]
    cols = noise_sigma.shape[2]
    elem_rows = rows // EL
    elem_cols = cols // EL
    shapes = corner_shapes(rows, cols)
    live_rows = jnp.repeat(crack_mask.astype(jnp.float32), 128, axis=1)
    pixel_scale = live_rows[None] / noise_sigma
    design = (
        shapes[:, None, None] * pixel_scale[None, None] * coefficients.astype(jnp.float32)[None]
    ).astype(jnp.bfloat16)
    design = design.reshape(4, 3, CAMS, elem_rows, EL, elem_cols, EL).transpose(0, 1, 3, 5, 2, 4, 6)
    design = design.reshape(12, elem_rows * elem_cols, CAMS * EL * EL)
    weighted = (pixel_scale * residual).astype(jnp.bfloat16)
    weighted = (
        weighted.reshape(CAMS, elem_rows, EL, elem_cols, EL).transpose(1, 3, 0, 2, 4).reshape(-1)
    )
    right_edge = shifted(node_panel[:, :1], "col", -1)
    widened = jnp.concatenate([node_panel, right_edge], axis=1)
    lower_edge = shifted(widened, "row", -1)
    extended = jnp.concatenate([widened, lower_edge], axis=0)
    own_rows = pixel_rows(design, extended)
    grad_part = jnp.dot(weighted, own_rows, preferred_element_type=jnp.float32)
    block = block_product(
        own_rows, pixel_rows(design, lax.all_gather(extended, "param", axis=3, tiled=True))
    )
    hessian, gradient = (
        lax.psum_scatter(block, ("row", "col"), scatter_dimension=1, tiled=True),
        lax.psum_scatter(grad_part, ("row", "col"), scatter_dimension=0, tiled=True),
    )
    return (hessian, gradient)


def solution(mesh):
    in_specs = (
        P(None, None, "row", "col"),
        P(None, "row", "col"),
        P(None, "row", "col"),
        P("row", "col"),
        P("row", "col", None, "param"),
    )
    out_specs = (P("param", ("row", "col")), P(("param", "row", "col")))
    return jax.shard_map(
        on_device, mesh=mesh, in_specs=in_specs, out_specs=out_specs, check_vma=False
    )
```

profile of v0, /device:TPU:29, one launch (start us, length us, event | category | flops | bytes accessed | tf_op | source)
XLA Modules:
  0.0 162.7 jit_solution(3008895666542584346)
XLA Ops:
  7.2 0.0 copy-start
  7.2 0.0 reduce-scatter.2.cloned.1.call-start
  7.2 0.8 slice.24
  8.0 2.6 %collective-permute-start = (bf16[1,1,3,1024]{3,1,2,0:T(2,128)(2,1)S(1)}, bf16[1,1,3,1024]{3,1,2,0:T(2,128)(2,1)S(1)}, u32[]{:S(2)}, u32[]{:S(2)}) collective-permute-start(bf16[1,1,3,1024]{3,1,2,0:T(2,128)(2,1)S(1)} %slice.24), channel_id=1, source_target_pairs={{1,0},{2,1},{3,2},{5,4},{6,5},{7,6},{9,8},{10,9},{11,10},{13,12},{... | collective-permute-start | bytes 18440 | tf_op jit(solution)/shard_map/ppermute | solution.py:13
  10.7 0.7 convert_bitcast_fusion
  11.3 0.8 multiply_convert_fusion.1
  12.1 0.1 mul.140
  12.2 0.1 copy.25
  12.3 0.9 reshape.255
  13.3 0.1 copy.26
  13.4 0.1 broadcast_multiply_fusion.3
  13.6 0.1 multiply_convert_fusion
  13.7 0.9 constant_dynamic-update-slice_fusion.1
  14.6 0.2 copy.27
  14.8 0.0 collective-permute-done
  14.8 2.1 %collective-permute-start.1 = (bf16[1,17,3,1024]{3,1,2,0:T(8,128)(2,1)S(1)}, bf16[1,17,3,1024]{3,1,2,0:T(8,128)(2,1)S(1)}, u32[]{:S(2)}, u32[]{:S(2)}) collective-permute-start(bf16[1,17,3,1024]{3,1,2,0:T(8,128)(2,1)S(1)} %constant_dynamic-update-slice_fusion), channel_id=1, source_target_pairs={{4,0},{8,4},{12,8},{5,1},{9,5},{13,9},{6,2},{10,6},{14,10},{7,3},{... | collective-permute-start | bytes 313352 | tf_op jit(solution)/shard_map/ppermute | solution.py:13
  16.9 3.2 %collective-permute-done.1 = bf16[1,17,3,1024]{3,1,2,0:T(8,128)(2,1)S(1)} collective-permute-done((bf16[1,17,3,1024]{3,1,2,0:T(8,128)(2,1)S(1)}, bf16[1,17,3,1024]{3,1,2,0:T(8,128)(2,1)S(1)}, u32[]{:S(2)}, u32[]{:S(2)}) %collective-permute-start.1) | collective-permute-done | bytes 104480 | tf_op jit(solution)/shard_map/ppermute | solution.py:13
  20.2 8.4 %all_gather.3 = bf16[2,17,3,2048]{3,1,2,0:T(8,128)(2,1)S(1)} all-gather(bf16[2,17,3,1024]{3,1,2,0:T(8,128)(2,1)S(1)} %pad_maximum_fusion.2), channel_id=1, replica_groups=mesh['param'=2,'row'=4,'col'=4] {'param'}, dimensions={3}, use_global_device_ids=true | all-gather | bytes 626688 | tf_op jit(solution)/shard_map/all_gather | solution.py:66
  28.6 0.1 slice_bitcast_fusion.3
  28.8 0.0 copy-done
  28.8 0.1 pad_maximum_fusion.1
  28.8 3.3 %convolution_convert_fusion = bf16[16,128,1024]{2,1,0:T(8,128)(2,1)} fusion(bf16[12,16,128]{2,0,1:T(8,128)(2,1)S(1)} %copy.27, bf16[16,12,1024]{2,0,1:T(8,128)(2,1)S(1)} %bitcast.38), kind=kOutput, calls=%fused_computation.3 | convolution fusion | flops 52428800 | bytes 4636672 | tf_op jit(solution)/shard_map/kep,ekq->epq/dot_general | solution.py:32
  32.1 0.1 pad_maximum_fusion
  32.2 16.6 %fusion.2 = f32[1024,2048]{1,0:T(8,128)} fusion(bf16[16,128,1024]{2,1,0:T(8,128)(2,1)} %convolution_convert_fusion, bf16[12,16,128]{2,0,1:T(8,128)(2,1)S(1)} %copy.27, bf16[16,12,2048]{2,0,1:T(8,128)(2,1)S(1)} %bitcast.40), kind=kOutput, calls=%fused_computation.2 | convolution fusion | flops 8694792192 | bytes 13418496 | tf_op jit(solution)/shard_map/dot_general | solution.py:37
  48.8 0.0 copy-start.1
  48.8 0.0 reduce-scatter.2.cloned.1.call-update
  48.8 0.1 reshape.252
  49.0 0.1 reshape.257
  49.1 0.4 copy-done.1
  49.4 0.6 dynamic-slice
  50.7 2.8 %fusion.21 = f32[1,1024]{1,0:T(1,128)S(1)} fusion(bf16[2048,1]{0,1:T(2,128)(2,1)S(1)} %reshape.257, bf16[2048,1024]{1,0:T(8,128)(2,1)} %bitcast.37), kind=kOutput, calls=%fused_computation.43 | convolution fusion | flops 4194304 | bytes 4202496 | tf_op jit(solution)/shard_map/dot_general | solution.py:64
  53.5 28.9 %all-reduce = f32[1024]{0:T(1024)S(1)} all-reduce(f32[1024]{0:T(1024)S(1)} %bitcast.43), channel_id=3, replica_groups=mesh['param'=2,'row'=4,'col'=4] {'row','col'}, use_global_device_ids=true, to_apply=%region_1.2.clone | all-reduce | flops 1024 | bytes 8192
  82.4 0.6 dynamic-slice.1
  83.0 72.8 %reduce-scatter.2.cloned.1.call-done = f32[1024,128]{1,0:T(8,128)} async-done(((f32[1024,2048]{1,0:T(8,128)}), f32[1024,128]{1,0:T(8,128)}) %reduce-scatter.2.cloned.1.call-update) | async-done | bytes 524304 | tf_op jit(solution)/shard_map/reduce_scatter | solution.py:69
  (9 shorter events, 0.2 us)
Async XLA Ops:
  7.2 21.6 %copy-start = (bf16[1,16,3,1024]{3,1,2,0:T(8,128)(2,1)S(1)}, bf16[1,16,3,1024]{3,1,2,0:T(8,128)(2,1)}, u32[]{:S(2)}) copy-start(bf16[1,16,3,1024]{3,1,2,0:T(8,128)(2,1)} %param.9) | copy-start | bytes 294916
  7.2 148.6 %reduce-scatter.2.cloned.1.call-start = ((), (), s32[]{:S(2)}) async-start(), calls=%async_computation.1 | async-start | bytes 8912896 | tf_op jit(solution)/shard_map/reduce_scatter | solution.py:69
  8.0 6.7 %collective-permute-start = (bf16[1,1,3,1024]{3,1,2,0:T(2,128)(2,1)S(1)}, bf16[1,1,3,1024]{3,1,2,0:T(2,128)(2,1)S(1)}, u32[]{:S(2)}, u32[]{:S(2)}) collective-permute-start(bf16[1,1,3,1024]{3,1,2,0:T(2,128)(2,1)S(1)} %slice.24), channel_id=1, source_target_pairs={{1,0},{2,1},{3,2},{5,4},{6,5},{7,6},{9,8},{10,9},{11,10},{13,12},{... | collective-permute-start | bytes 18440 | tf_op jit(solution)/shard_map/ppermute | solution.py:13
  14.8 5.3 %collective-permute-start.1 = (bf16[1,17,3,1024]{3,1,2,0:T(8,128)(2,1)S(1)}, bf16[1,17,3,1024]{3,1,2,0:T(8,128)(2,1)S(1)}, u32[]{:S(2)}, u32[]{:S(2)}) collective-permute-start(bf16[1,17,3,1024]{3,1,2,0:T(8,128)(2,1)S(1)} %constant_dynamic-update-slice_fusion), channel_id=1, source_target_pairs={{4,0},{8,4},{12,8},{5,1},{9,5},{13,9},{6,2},{10,6},{14,10},{7,3},{... | collective-permute-start | bytes 313352 | tf_op jit(solution)/shard_map/ppermute | solution.py:13
  48.8 0.7 copy-start.1
Sparse Core Ops, SparseCore 0:
  48.9 106.8 reduce-scatter.1
where the time goes:
time: 166 us; the launch traced here: 163 us
  waiting for transfers between devices  76 us (46%)
  blocking collectives  37.3 us (22%)
  matrix products  22.7 us (14%)
  between operations  14.9 us (9%)
  local copies, waits for them, and re-layouts  5.19 us (3%)
  starting transfers between devices  4.7 us (3%)
  other arithmetic  1.87 us (1%)
    reduce_scatter x1, waiting for transfers between devices, on_device(): lax.psum_scatter(block, ('row', 'col'), scatter_dimension=1, tiled=True)  72.8 us
    unnamed x1, blocking collectives  28.9 us
    dot_general x1, matrix products, block_product(): lax.dot_general(own_rows, other_rows, (((0,), (0,)), ((), ())), preferred...  16.6 us
    all_gather x1, blocking collectives, on_device(): lax.all_gather(extended, 'param', axis=3, tiled=True)  8.42 us
    ppermute x2, starting transfers between devices, shifted(): return lax.ppermute(block, axis, route)  4.66 us
  transfers between devices with their start and end apart: 3, of which 2 were waited for; matrix products, arithmetic and copies ran while one was open for 5% of the time, Pallas kernels for 0%

commit v1 on v0

--- a/solution.py
+++ b/solution.py
@@ -1,10 +1,20 @@
+import functools
+
 import jax
 import jax.numpy as jnp
 from jax import lax
+from jax.experimental import pallas as pl
+from jax.experimental.pallas import tpu as pltpu
 from jax.sharding import PartitionSpec as P
 
 EL = 8
 CAMS = 2
+CORNERS = ((0, 0), (0, 1), (1, 0), (1, 1))
+PAIRS = [(i, j) for i in range(12) for j in range(i, 12)]
+PAIR_ROW = {pair: row for row, pair in enumerate(PAIRS)}
+FORCE_ROW = len(PAIRS)
+UP, DOWN, ACROSS, CORE, PEER = range(5)
+MESH = pl.DeviceIdType.MESH
 
 
 def shifted(block, axis, distance):
@@ -39,7 +49,7 @@
     )
 
 
-def on_device(coefficients, noise_sigma, residual, crack_mask, node_panel):
+def plain(coefficients, noise_sigma, residual, crack_mask, node_panel):
     rows = noise_sigma.shape[1]
     cols = noise_sigma.shape[2]
     elem_rows = rows // EL
@@ -65,14 +75,294 @@
     block = block_product(
         own_rows, pixel_rows(design, lax.all_gather(extended, "param", axis=3, tiled=True))
     )
-    hessian, gradient = (
+    return (
         lax.psum_scatter(block, ("row", "col"), scatter_dimension=1, tiled=True),
         lax.psum_scatter(grad_part, ("row", "col"), scatter_dimension=0, tiled=True),
     )
-    return (hessian, gradient)
+
+
+def element_grams(coef_ref, sigma_ref, resid_ref, mask_ref):
+    live = jnp.broadcast_to(mask_ref[...].astype(jnp.float32), (8, 128))
+    y = lax.broadcasted_iota(jnp.int32, (8, 128), 0).astype(jnp.float32)
+    x = (lax.broadcasted_iota(jnp.int32, (8, 128), 1) % EL).astype(jnp.float32)
+    v = (y + 0.5) / EL
+    u = (x + 0.5) / EL
+    scale = [live / sigma_ref[c] for c in range(CAMS)]
+
+    def rounded(value):
+        return value.astype(jnp.bfloat16).astype(jnp.float32)
+
+    coef = [[coef_ref[k, c].astype(jnp.float32) for c in range(CAMS)] for k in range(3)]
+    weighted = [rounded(scale[c] * resid_ref[c]) for c in range(CAMS)]
+    design = []
+    for a, b in CORNERS:
+        shape = (v if a else 1.0 - v) * (u if b else 1.0 - u)
+        placed = [shape * scale[c] for c in range(CAMS)]
+        for k in range(3):
+            design.append([rounded(placed[c] * coef[k][c]) for c in range(CAMS)])
+
+    def row(one, other):
+        total = one[0] * other[0] + one[1] * other[1]
+        return jnp.sum(total, axis=0, keepdims=True)
+
+    rows = [row(design[i], design[j]) for i, j in PAIRS]
+    rows += [row(design[i], weighted) for i in range(12)]
+    rows.append(jnp.zeros((128 - len(rows), 128), jnp.float32))
+    sums = jnp.concatenate(rows, axis=0)
+    element = lax.broadcasted_iota(jnp.int32, (16, 128), 0)
+    pixel = lax.broadcasted_iota(jnp.int32, (16, 128), 1)
+    segment = (pixel // EL == element).astype(jnp.float32)
+    return lax.dot_general(
+        segment, sums, (((1,), (1,)), ((), ())),
+        precision=lax.Precision.HIGHEST, preferred_element_type=jnp.float32,
+    )
+
+
+def assemble(grams_ref, moved_ref, stiff_ref, wide_ref, nodes, width):
+    turned = grams_ref[...].T
+    node = lax.broadcasted_iota(jnp.int32, (1, nodes), 1)
+    node_row, node_col = node // width, node % width
+    for n, (a, b) in enumerate(CORNERS):
+        ok = (node_row >= a) & (node_col >= b)
+        shift = a * width + b
+        moved = pltpu.roll(turned, shift, 1) if shift else turned
+        moved_ref[n] = jnp.where(ok, moved, 0.0)
+    has_right = node_col < width - 1
+
+    def gram_row(n, k, m, l):
+        i, j = 3 * n + k, 3 * m + l
+        return moved_ref[m, pl.ds(PAIR_ROW[(min(i, j), max(i, j))], 1), :]
+
+    place = lax.broadcasted_iota(jnp.int32, (nodes, nodes), 0) - lax.broadcasted_iota(
+        jnp.int32, (nodes, nodes), 1
+    )
+    for k in range(3):
+        for l in range(3):
+            bands = {}
+            for n, (a, b) in enumerate(CORNERS):
+                for m, (a2, b2) in enumerate(CORNERS):
+                    term = gram_row(n, k, m, l)
+                    if b > b2:
+                        term = jnp.where(has_right, term, 0.0)
+                    offset = (a - a2) * width + b - b2
+                    bands[offset] = bands[offset] + term if offset in bands else term
+            block = jnp.zeros((nodes, nodes), jnp.float32)
+            for offset, band in bands.items():
+                block = jnp.where(place == offset, band, block)
+            stiff_ref[k * nodes:(k + 1) * nodes, l * nodes:(l + 1) * nodes] = block.astype(
+                jnp.bfloat16
+            )
+    parts = []
+    for k in range(3):
+        force = moved_ref[0, pl.ds(FORCE_ROW + k, 1), :]
+        for m in range(1, 4):
+            force = force + moved_ref[m, pl.ds(FORCE_ROW + 3 * m + k, 1), :]
+        parts.append(force)
+    force = jnp.concatenate(parts, axis=1)
+    high = force.astype(jnp.bfloat16).astype(jnp.float32)
+    low = force - high
+    which = lax.broadcasted_iota(jnp.int32, (16, 3 * nodes), 0)
+    wide_ref[128:144, :] = jnp.where(
+        which == 0, high, jnp.where(which == 1, low, 0.0)
+    ).astype(jnp.bfloat16)
+
+
+def kernel(
+    sizes, coef_ref, sigma_ref, resid_ref, mask_ref, panel_ref, hess_ref, grad_ref,
+    held, picked, grams, moved, stiff, wide, line,
+    send_sem, recv_sem, gram_send, gram_recv, peer_recv,
+):
+    depth, columns, share = sizes
+    tiles = depth * columns
+    nodes = tiles * 16
+    width = columns * 16
+    param, z, col = lax.axis_index("param"), lax.axis_index("row"), lax.axis_index("col")
+    y, c = col // 2, col % 2
+    mine = z * columns + col
+    per_share = share // 128
+    owner = mine // per_share
+    is_owner = owner == param
+    first_column = pl.multiple_of((mine % per_share) * 128, 128)
+    targets = {
+        UP: (param, z + 1, col),
+        DOWN: (param, z - 1, col),
+        ACROSS: (param, z, (1 - y) * 2 + c),
+        CORE: (param, z, y * 2 + 1 - c),
+        PEER: (1 - param, z, col),
+    }
+    exists = {UP: z < depth - 1, DOWN: z > 0}
+
+    def tile(zz, yy, cc):
+        return zz * columns + yy * 2 + cc
+
+    def rows_of(t):
+        return pl.ds(pl.multiple_of(t * 16, 16), 16)
+
+    def block_copy(t, way):
+        if way == PEER:
+            return pltpu.make_async_remote_copy(
+                src_ref=held.at[:, rows_of(t), pl.ds(first_column, 128)],
+                dst_ref=picked.at[:, rows_of(t), :],
+                send_sem=send_sem.at[way, t], recv_sem=peer_recv.at[t],
+                device_id=targets[way], device_id_type=MESH,
+            )
+        return pltpu.make_async_remote_copy(
+            src_ref=held.at[:, rows_of(t), :], dst_ref=held.at[:, rows_of(t), :],
+            send_sem=send_sem.at[way, t], recv_sem=recv_sem.at[t],
+            device_id=targets[way], device_id_type=MESH,
+        )
+
+    def gram_copy(t, way):
+        return pltpu.make_async_remote_copy(
+            src_ref=grams.at[rows_of(t), :], dst_ref=grams.at[rows_of(t), :],
+            send_sem=gram_send.at[way, t], recv_sem=gram_recv.at[t],
+            device_id=targets[way], device_id_type=MESH,
+        )
+
+    def guarded(condition, action):
+        if condition is None:
+            action()
+        else:
+            pl.when(condition)(action)
+
+    sent = []
+
+    def both(one, other):
+        if one is None:
+            return other
+        return one if other is None else one & other
+
+    def send_block(t, ways, condition=None):
+        for way in ways:
+            when = both(condition, exists.get(way))
+            guarded(when, lambda: block_copy(t, way).start())
+            sent.append((when, block_copy, t, way))
+        when = both(condition, is_owner)
+        guarded(when, lambda: block_copy(t, PEER).start())
+        sent.append((when, block_copy, t, PEER))
+
+    def send_gram(t, ways, condition=None):
+        for way in ways:
+            when = both(condition, exists.get(way))
+            guarded(when, lambda: gram_copy(t, way).start())
+            sent.append((when, gram_copy, t, way))
+
+    def pass_on(t, ways, condition=None):
+        guarded(condition, lambda: block_copy(t, CORE).wait_recv())
+        send_block(t, ways, condition)
+        guarded(condition, lambda: gram_copy(t, CORE).wait_recv())
+        send_gram(t, ways, condition)
+
+    barrier = pltpu.get_barrier_semaphore()
+    for way in range(5):
+        guarded(
+            exists.get(way),
+            lambda: pl.semaphore_signal(
+                barrier, inc=1, device_id=targets[way], device_id_type=MESH
+            ),
+        )
+    held[:, rows_of(mine), :] = panel_ref[...]
+    partners = 3 + jnp.where(z > 0, 1, 0) + jnp.where(z < depth - 1, 1, 0)
+    pl.semaphore_wait(barrier, partners)
+
+    send_block(mine, (UP, DOWN, ACROSS, CORE))
+    grams[rows_of(mine), :] = element_grams(coef_ref, sigma_ref, resid_ref, mask_ref)
+    send_gram(mine, (UP, DOWN, ACROSS, CORE))
+
+    pass_on(tile(z, 1 - y, c), (CORE,))
+    for k in range(1, depth):
+        below, above = z - k >= 0, z + k < depth
+        pass_on(tile(z - k, y, c), (UP, ACROSS, CORE), below)
+        pass_on(tile(z + k, y, c), (DOWN, ACROSS, CORE), above)
+        if k > 1:
+            pass_on(tile(z - k + 1, 1 - y, c), (CORE,), z - k + 1 >= 0)
+            pass_on(tile(z + k - 1, 1 - y, c), (CORE,), z + k - 1 < depth)
+    k = depth
+    pass_on(tile(z - k + 1, 1 - y, c), (CORE,), z - k + 1 >= 0)
+    pass_on(tile(z + k - 1, 1 - y, c), (CORE,), z + k - 1 < depth)
+    for zz in range(depth):
+        for yy in range(2):
+            pass_on(tile(zz, yy, 1 - c), ())
+
+    assemble(grams, moved, stiff, wide, nodes, width)
+
+    @pl.when(is_owner)
+    def _():
+        picked[...] = held[:, :, pl.ds(first_column, 128)]
+
+    @pl.when(jnp.logical_not(is_owner))
+    def _():
+        for t in range(tiles):
+            block_copy(t, PEER).wait_recv()
+
+    chosen = picked[...].reshape(3 * nodes, 128)
+    turned = lax.dot_general(
+        chosen, stiff[...], (((0,), (0,)), ((), ())), preferred_element_type=jnp.float32
+    )
+    wide[0:128, :] = turned.astype(jnp.bfloat16)
+    product = jnp.dot(
+        wide[...], held[...].reshape(3 * nodes, share), preferred_element_type=jnp.float32
+    )
+    hess_ref[...] = product[:128].T
+    line[...] = jnp.broadcast_to(product[128:129] + product[129:130], (8, share))
+    pair = line[0:1, pl.ds(pl.multiple_of((mine // 2) * 128, 128), 128)]
+    pair = jnp.where(mine % 2 == 1, pltpu.roll(pair, 64, 1), pair)
+    grad_ref[...] = pair[:, :64]
+
+    for when, copy, t, way in sent:
+        guarded(when, lambda: copy(t, way).wait_send())
+
+
+def gathered(sizes, coefficients, noise_sigma, residual, crack_mask, node_panel):
+    depth, columns, share = sizes
+    tiles = depth * columns
+    nodes = tiles * 16
+    panel = node_panel[0].transpose(1, 0, 2)
+    hessian, gradient = pl.pallas_call(
+        functools.partial(kernel, sizes),
+        out_shape=(
+            jax.ShapeDtypeStruct((share, 128), jnp.float32),
+            jax.ShapeDtypeStruct((1, 64), jnp.float32),
+        ),
+        in_specs=[pl.BlockSpec(memory_space=pltpu.VMEM)] * 5,
+        out_specs=[pl.BlockSpec(memory_space=pltpu.VMEM)] * 2,
+        scratch_shapes=[
+            pltpu.VMEM((3, nodes, share), jnp.bfloat16),
+            pltpu.VMEM((3, nodes, 128), jnp.bfloat16),
+            pltpu.VMEM((nodes, 128), jnp.float32),
+            pltpu.VMEM((4, 128, nodes), jnp.float32),
+            pltpu.VMEM((3 * nodes, 3 * nodes), jnp.bfloat16),
+            pltpu.VMEM((144, 3 * nodes), jnp.bfloat16),
+            pltpu.VMEM((8, share), jnp.float32),
+            pltpu.SemaphoreType.DMA((5, tiles)),
+            pltpu.SemaphoreType.DMA((tiles,)),
+            pltpu.SemaphoreType.DMA((4, tiles)),
+            pltpu.SemaphoreType.DMA((tiles,)),
+            pltpu.SemaphoreType.DMA((tiles,)),
+        ],
+        compiler_params=pltpu.CompilerParams(
+            collective_id=0, has_side_effects=True, vmem_limit_bytes=32 * 2**20
+        ),
+    )(coefficients, noise_sigma, residual, crack_mask, panel)
+    return hessian, gradient.reshape(64)
 
 
 def solution(mesh):
+    def on_device(coefficients, noise_sigma, residual, crack_mask, node_panel):
+        depth, columns, share = mesh.shape["row"], mesh.shape["col"], node_panel.shape[3]
+        fits = (
+            mesh.shape["param"] == 2
+            and columns == 4
+            and noise_sigma.shape == (CAMS, EL, 128)
+            and node_panel.shape[:3] == (1, 16, 3)
+            and share == 64 * depth * columns
+        )
+        if fits:
+            return gathered(
+                (depth, columns, share), coefficients, noise_sigma, residual, crack_mask, node_panel
+            )
+        return plain(coefficients, noise_sigma, residual, crack_mask, node_panel)
+
     in_specs = (
         P(None, None, "row", "col"),
         P(None, "row", "col"),

time: 166 us -> 30.2 us (0.18)
  the two profiles are of different devices: /device:TPU:29 before, /device:TPU:2 now
where the time goes in v1:
time: 30.2 us; the launch traced here: 29.8 us
  Pallas kernels  24.2 us (80%)
  local copies, waits for them, and re-layouts  5.03 us (17%)
  between operations  0.65 us (2%)
    pallas_call x1, Pallas kernels, gathered(): pl.pallas_call(functools.partial(kernel, sizes), out_shape=(jax.ShapeDtyp...  24.2 us
    unnamed x13, local copies, waits for them, and re-layouts  5.03 us

profile of v1, /device:TPU:2, one launch (start us, length us, event | category | flops | bytes accessed | tf_op | source)
XLA Modules:
  0.0 29.8 jit_solution(166151475395084121)
XLA Ops:
  0.6 0.0 copy-start.4
  0.6 0.6 %copy-done.4 = s32[8,1]{0,1:T(1,128)S(1)} copy-done((s32[8,1]{0,1:T(1,128)S(1)}, s32[8,1]{0,1:T(1,128)}, u32[]{:S(2)}) %copy-start.4) | copy-done | bytes 56
  1.3 0.1 copy.7.mask_ref
  1.4 0.0 copy-start
  1.4 0.9 %copy-done = bf16[1,16,3,1024]{3,1,2,0:T(8,128)(2,1)S(1)} copy-done((bf16[1,16,3,1024]{3,1,2,0:T(8,128)(2,1)S(1)}, bf16[1,16,3,1024]{3,1,2,0:T(8,128)(2,1)}, u32[]{:S(2)}) %copy-start) | copy-done | bytes 98328
  2.3 0.0 copy-start.1
  2.3 0.7 %copy-done.1 = bf16[3,2,8,128]{3,2,1,0:T(8,128)(2,1)S(1)} copy-done((bf16[3,2,8,128]{3,2,1,0:T(8,128)(2,1)S(1)}, bf16[3,2,8,128]{3,2,1,0:T(8,128)(2,1)}, u32[]{:S(2)}) %copy-start.1) | copy-done | bytes 12312
  3.0 0.0 copy-start.2
  3.0 0.7 %copy-done.2 = f32[2,8,128]{2,1,0:T(8,128)S(1)} copy-done((f32[2,8,128]{2,1,0:T(8,128)S(1)}, f32[2,8,128]{2,1,0:T(8,128)}, u32[]{:S(2)}) %copy-start.2) | copy-done | bytes 8216
  3.7 0.0 copy-start.3
  3.7 0.7 %copy-done.3 = f32[2,8,128]{2,1,0:T(8,128)S(1)} copy-done((f32[2,8,128]{2,1,0:T(8,128)S(1)}, f32[2,8,128]{2,1,0:T(8,128)}, u32[]{:S(2)}) %copy-start.3) | copy-done | bytes 8216
  4.4 24.2 %shard_map.68 = (f32[1024,128]{1,0:T(8,128)S(1)}, f32[1,64]{1,0:T(1,128)S(1)}) custom-call(bf16[3,2,8,128]{3,2,1,0:T(8,128)(2,1)S(1)} %copy-done.1, f32[2,8,128]{2,1,0:T(8,128)S(1)} %copy-done.2, f32[2,8,128]{2,1,0:T(8,128)S(1)} %copy-done.3, s32[8,1]{1,0:T(8,128)S(1)} %copy.7.mask_ref, bf16[3,16,1024]{2,1,0:T(8,128)(2,1)S(1)} %bitcast.4), custom_call_target="tpu_custom_call" | custom-call | tf_op jit(solution)/shard_map/pallas_call | solution.py:321
  28.5 0.8 %copy.10 = f32[1024,128]{1,0:T(8,128)} copy(f32[1024,128]{1,0:T(8,128)S(1)} %get-tuple-element.8) | data formatting | bytes 1048576
  29.3 0.5 %copy.11 = f32[64]{0:T(128)} copy(f32[64]{0:T(128)S(1)} %bitcast.5) | data formatting | bytes 512
Async XLA Ops:
  0.6 0.7 %copy-start.4 = (s32[8,1]{0,1:T(1,128)S(1)}, s32[8,1]{0,1:T(1,128)}, u32[]{:S(2)}) copy-start(s32[8,1]{0,1:T(1,128)} %param.8) | copy-start | bytes 100
  1.4 0.9 %copy-start = (bf16[1,16,3,1024]{3,1,2,0:T(8,128)(2,1)S(1)}, bf16[1,16,3,1024]{3,1,2,0:T(8,128)(2,1)}, u32[]{:S(2)}) copy-start(bf16[1,16,3,1024]{3,1,2,0:T(8,128)(2,1)} %param.9) | copy-start | bytes 294916
  2.3 0.7 %copy-start.1 = (bf16[3,2,8,128]{3,2,1,0:T(8,128)(2,1)S(1)}, bf16[3,2,8,128]{3,2,1,0:T(8,128)(2,1)}, u32[]{:S(2)}) copy-start(bf16[3,2,8,128]{3,2,1,0:T(8,128)(2,1)} %coef_ref.1) | copy-start | bytes 36868
  3.0 0.7 %copy-start.2 = (f32[2,8,128]{2,1,0:T(8,128)S(1)}, f32[2,8,128]{2,1,0:T(8,128)}, u32[]{:S(2)}) copy-start(f32[2,8,128]{2,1,0:T(8,128)} %sigma_ref.1) | copy-start | bytes 24580
  3.7 0.7 %copy-start.3 = (f32[2,8,128]{2,1,0:T(8,128)S(1)}, f32[2,8,128]{2,1,0:T(8,128)}, u32[]{:S(2)}) copy-start(f32[2,8,128]{2,1,0:T(8,128)} %resid_ref.1) | copy-start | bytes 24580

commit v2 on v1

--- a/solution.py
+++ b/solution.py
@@ -82,7 +82,10 @@
 
 
 def element_grams(coef_ref, sigma_ref, resid_ref, mask_ref):
-    live = jnp.broadcast_to(mask_ref[...].astype(jnp.float32), (8, 128))
+    mask = jnp.broadcast_to(mask_ref[...].astype(jnp.float32), (8, 8))
+    own = lax.broadcasted_iota(jnp.int32, (8, 8), 0) == lax.broadcasted_iota(jnp.int32, (8, 8), 1)
+    live = jnp.sum(jnp.where(own, mask, 0.0), axis=1, keepdims=True)
+    live = jnp.broadcast_to(live, (8, 128))
     y = lax.broadcasted_iota(jnp.int32, (8, 128), 0).astype(jnp.float32)
     x = (lax.broadcasted_iota(jnp.int32, (8, 128), 1) % EL).astype(jnp.float32)
     v = (y + 0.5) / EL
@@ -118,7 +121,7 @@
     )
 
 
-def assemble(grams_ref, moved_ref, stiff_ref, wide_ref, nodes, width):
+def corner_moves(grams_ref, moved_ref, wide_ref, nodes, width):
     turned = grams_ref[...].T
     node = lax.broadcasted_iota(jnp.int32, (1, nodes), 1)
     node_row, node_col = node // width, node % width
@@ -127,31 +130,6 @@
         shift = a * width + b
         moved = pltpu.roll(turned, shift, 1) if shift else turned
         moved_ref[n] = jnp.where(ok, moved, 0.0)
-    has_right = node_col < width - 1
-
-    def gram_row(n, k, m, l):
-        i, j = 3 * n + k, 3 * m + l
-        return moved_ref[m, pl.ds(PAIR_ROW[(min(i, j), max(i, j))], 1), :]
-
-    place = lax.broadcasted_iota(jnp.int32, (nodes, nodes), 0) - lax.broadcasted_iota(
-        jnp.int32, (nodes, nodes), 1
-    )
-    for k in range(3):
-        for l in range(3):
-            bands = {}
-            for n, (a, b) in enumerate(CORNERS):
-                for m, (a2, b2) in enumerate(CORNERS):
-                    term = gram_row(n, k, m, l)
-                    if b > b2:
-                        term = jnp.where(has_right, term, 0.0)
-                    offset = (a - a2) * width + b - b2
-                    bands[offset] = bands[offset] + term if offset in bands else term
-            block = jnp.zeros((nodes, nodes), jnp.float32)
-            for offset, band in bands.items():
-                block = jnp.where(place == offset, band, block)
-            stiff_ref[k * nodes:(k + 1) * nodes, l * nodes:(l + 1) * nodes] = block.astype(
-                jnp.bfloat16
-            )
     parts = []
     for k in range(3):
         force = moved_ref[0, pl.ds(FORCE_ROW + k, 1), :]
@@ -167,10 +145,38 @@
     ).astype(jnp.bfloat16)
 
 
+def assemble(moved_ref, stiff_ref, nodes, width, blocks):
+    node_col = lax.broadcasted_iota(jnp.int32, (1, nodes), 1) % width
+    has_right = node_col < width - 1
+
+    def gram_row(n, k, m, l):
+        i, j = 3 * n + k, 3 * m + l
+        return moved_ref[m, pl.ds(PAIR_ROW[(min(i, j), max(i, j))], 1), :]
+
+    place = lax.broadcasted_iota(jnp.int32, (nodes, nodes), 0) - lax.broadcasted_iota(
+        jnp.int32, (nodes, nodes), 1
+    )
+    for k, l in blocks:
+        bands = {}
+        for n, (a, b) in enumerate(CORNERS):
+            for m, (a2, b2) in enumerate(CORNERS):
+                term = gram_row(n, k, m, l)
+                if b > b2:
+                    term = jnp.where(has_right, term, 0.0)
+                offset = (a - a2) * width + b - b2
+                bands[offset] = bands[offset] + term if offset in bands else term
+        block = jnp.zeros((nodes, nodes), jnp.float32)
+        for offset, band in bands.items():
+            block = jnp.where(place == offset, band, block)
+        stiff_ref[k * nodes:(k + 1) * nodes, l * nodes:(l + 1) * nodes] = block.astype(
+            jnp.bfloat16
+        )
+
+
 def kernel(
-    sizes, coef_ref, sigma_ref, resid_ref, mask_ref, panel_ref, hess_ref, grad_ref,
-    held, picked, grams, moved, stiff, wide, line,
-    send_sem, recv_sem, gram_send, gram_recv, peer_recv,
+    sizes, coef_hbm, sigma_hbm, resid_hbm, mask_hbm, panel_hbm, hess_ref, grad_ref,
+    coef_ref, sigma_ref, resid_ref, mask_ref, held, picked, grams, moved, stiff, wide, line,
+    load_sem, send_sem, recv_sem, gram_send, gram_recv, peer_recv,
 ):
     depth, columns, share = sizes
     tiles = depth * columns
@@ -212,11 +218,15 @@
             device_id=targets[way], device_id_type=MESH,
         )
 
-    def gram_copy(t, way):
+    def peer_of(step):
+        other = lax.rem(mine + step, tiles)
+        return other, (param, other // columns, other % columns)
+
+    def gram_copy(t, step):
         return pltpu.make_async_remote_copy(
             src_ref=grams.at[rows_of(t), :], dst_ref=grams.at[rows_of(t), :],
-            send_sem=gram_send.at[way, t], recv_sem=gram_recv.at[t],
-            device_id=targets[way], device_id_type=MESH,
+            send_sem=gram_send.at[step], recv_sem=gram_recv.at[t],
+            device_id=peer_of(step)[1], device_id_type=MESH,
         )
 
     def guarded(condition, action):
@@ -241,34 +251,34 @@
         guarded(when, lambda: block_copy(t, PEER).start())
         sent.append((when, block_copy, t, PEER))
 
-    def send_gram(t, ways, condition=None):
-        for way in ways:
-            when = both(condition, exists.get(way))
-            guarded(when, lambda: gram_copy(t, way).start())
-            sent.append((when, gram_copy, t, way))
-
     def pass_on(t, ways, condition=None):
         guarded(condition, lambda: block_copy(t, CORE).wait_recv())
         send_block(t, ways, condition)
-        guarded(condition, lambda: gram_copy(t, CORE).wait_recv())
-        send_gram(t, ways, condition)
-
+
+    loads = [
+        pltpu.make_async_copy(panel_hbm, held.at[:, rows_of(mine), :], load_sem.at[0]),
+        pltpu.make_async_copy(mask_hbm, mask_ref, load_sem.at[1]),
+        pltpu.make_async_copy(sigma_hbm, sigma_ref, load_sem.at[2]),
+        pltpu.make_async_copy(coef_hbm, coef_ref, load_sem.at[3]),
+        pltpu.make_async_copy(resid_hbm, resid_ref, load_sem.at[4]),
+    ]
+    for load in loads:
+        load.start()
     barrier = pltpu.get_barrier_semaphore()
-    for way in range(5):
-        guarded(
-            exists.get(way),
-            lambda: pl.semaphore_signal(
-                barrier, inc=1, device_id=targets[way], device_id_type=MESH
-            ),
-        )
-    held[:, rows_of(mine), :] = panel_ref[...]
-    partners = 3 + jnp.where(z > 0, 1, 0) + jnp.where(z < depth - 1, 1, 0)
-    pl.semaphore_wait(barrier, partners)
+    pl.semaphore_signal(barrier, inc=1, device_id=targets[PEER], device_id_type=MESH)
+    for step in range(1, tiles):
+        pl.semaphore_signal(barrier, inc=1, device_id=peer_of(step)[1], device_id_type=MESH)
+    loads[0].wait()
+    pl.semaphore_wait(barrier, tiles)
 
     send_block(mine, (UP, DOWN, ACROSS, CORE))
+    for load in loads[1:]:
+        load.wait()
     grams[rows_of(mine), :] = element_grams(coef_ref, sigma_ref, resid_ref, mask_ref)
-    send_gram(mine, (UP, DOWN, ACROSS, CORE))
-
+    for step in range(1, tiles):
+        gram_copy(mine, step).start()
+
+    pairs = [(k, l) for k in range(3) for l in range(3)]
     pass_on(tile(z, 1 - y, c), (CORE,))
     for k in range(1, depth):
         below, above = z - k >= 0, z + k < depth
@@ -277,6 +287,12 @@
         if k > 1:
             pass_on(tile(z - k + 1, 1 - y, c), (CORE,), z - k + 1 >= 0)
             pass_on(tile(z + k - 1, 1 - y, c), (CORE,), z + k - 1 < depth)
+        if k == 2:
+            for step in range(1, tiles):
+                gram_copy(peer_of(step)[0], step).wait_recv()
+            corner_moves(grams, moved, wide, nodes, width)
+            assemble(moved, stiff, nodes, width, pairs[:4])
+    assemble(moved, stiff, nodes, width, pairs[4:])
     k = depth
     pass_on(tile(z - k + 1, 1 - y, c), (CORE,), z - k + 1 >= 0)
     pass_on(tile(z + k - 1, 1 - y, c), (CORE,), z + k - 1 < depth)
@@ -284,8 +300,6 @@
         for yy in range(2):
             pass_on(tile(zz, yy, 1 - c), ())
 
-    assemble(grams, moved, stiff, wide, nodes, width)
-
     @pl.when(is_owner)
     def _():
         picked[...] = held[:, :, pl.ds(first_column, 128)]
@@ -311,6 +325,19 @@
 
     for when, copy, t, way in sent:
         guarded(when, lambda: copy(t, way).wait_send())
+    for step in range(1, tiles):
+        gram_copy(mine, step).wait_send()
+
+
+def hand_over(hess_ref, grad_ref, hess_out, grad_out, sem):
+    copies = (
+        pltpu.make_async_copy(hess_ref, hess_out, sem.at[0]),
+        pltpu.make_async_copy(grad_ref, grad_out, sem.at[1]),
+    )
+    for copy in copies:
+        copy.start()
+    for copy in copies:
+        copy.wait()
 
 
 def gathered(sizes, coefficients, noise_sigma, residual, crack_mask, node_panel):
@@ -324,9 +351,13 @@
             jax.ShapeDtypeStruct((share, 128), jnp.float32),
             jax.ShapeDtypeStruct((1, 64), jnp.float32),
         ),
-        in_specs=[pl.BlockSpec(memory_space=pltpu.VMEM)] * 5,
+        in_specs=[pl.BlockSpec(memory_space=pltpu.HBM)] * 5,
         out_specs=[pl.BlockSpec(memory_space=pltpu.VMEM)] * 2,
         scratch_shapes=[
+            pltpu.VMEM(coefficients.shape, jnp.bfloat16),
+            pltpu.VMEM(noise_sigma.shape, jnp.float32),
+            pltpu.VMEM(residual.shape, jnp.float32),
+            pltpu.VMEM((1, EL), jnp.int32),
             pltpu.VMEM((3, nodes, share), jnp.bfloat16),
             pltpu.VMEM((3, nodes, 128), jnp.bfloat16),
             pltpu.VMEM((nodes, 128), jnp.float32),
@@ -334,16 +365,28 @@
             pltpu.VMEM((3 * nodes, 3 * nodes), jnp.bfloat16),
             pltpu.VMEM((144, 3 * nodes), jnp.bfloat16),
             pltpu.VMEM((8, share), jnp.float32),
+            pltpu.SemaphoreType.DMA((5,)),
             pltpu.SemaphoreType.DMA((5, tiles)),
             pltpu.SemaphoreType.DMA((tiles,)),
-            pltpu.SemaphoreType.DMA((4, tiles)),
+            pltpu.SemaphoreType.DMA((tiles,)),
             pltpu.SemaphoreType.DMA((tiles,)),
             pltpu.SemaphoreType.DMA((tiles,)),
         ],
         compiler_params=pltpu.CompilerParams(
-            collective_id=0, has_side_effects=True, vmem_limit_bytes=32 * 2**20
+            collective_id=0, has_side_effects=True, vmem_limit_bytes=60 * 2**20
         ),
-    )(coefficients, noise_sigma, residual, crack_mask, panel)
+    )(coefficients, noise_sigma, residual, crack_mask.reshape(1, EL), panel)
+    hessian, gradient = pl.pallas_call(
+        hand_over,
+        out_shape=(
+            jax.ShapeDtypeStruct((share, 128), jnp.float32),
+            jax.ShapeDtypeStruct((1, 64), jnp.float32),
+        ),
+        in_specs=[pl.BlockSpec(memory_space=pltpu.HBM)] * 2,
+        out_specs=[pl.BlockSpec(memory_space=pltpu.HBM)] * 2,
+        scratch_shapes=[pltpu.SemaphoreType.DMA((2,))],
+        compiler_params=pltpu.CompilerParams(vmem_limit_bytes=60 * 2**20),
+    )(hessian, gradient)
     return hessian, gradient.reshape(64)
 
 
@@ -353,6 +396,7 @@
         fits = (
             mesh.shape["param"] == 2
             and columns == 4
+            and depth >= 3
             and noise_sigma.shape == (CAMS, EL, 128)
             and node_panel.shape[:3] == (1, 16, 3)
             and share == 64 * depth * columns

time: 30.2 us -> 44.5 us (1.47)
  the two profiles are of different devices: /device:TPU:2 before, /device:TPU:29 now
where the time goes in v2:
time: 44.5 us; the launch traced here: 44.3 us
  Pallas kernels  43.7 us (98%)
  between operations  0.64 us (1%)
    pallas_call x1, Pallas kernels, gathered(): pl.pallas_call(functools.partial(kernel, sizes), out_shape=(jax.ShapeDtyp...  26.7 us
    pallas_call x1, Pallas kernels, gathered(): pl.pallas_call(hand_over, out_shape=(jax.ShapeDtypeStruct((share, 128), j...  17 us

profile of v2, /device:TPU:29, one launch (start us, length us, event | category | flops | bytes accessed | tf_op | source)
XLA Modules:
  0.0 44.3 jit_solution(17408039735372449706)
XLA Ops:
  0.6 26.7 %shard_map.68 = (f32[1024,128]{1,0:T(8,128)}, f32[1,64]{1,0:T(1,128)}) custom-call(bf16[3,2,8,128]{3,2,1,0:T(8,128)(2,1)} %coef_hbm.1, f32[2,8,128]{2,1,0:T(8,128)} %sigma_hbm.1, f32[2,8,128]{2,1,0:T(8,128)} %resid_hbm.1, s32[1,8]{1,0:T(1,128)} %bitcast.6, bf16[3,16,1024]{2,1,0:T(8,128)(2,1)} %bitcast.5), custom_call_target="tpu_custom_call" | custom-call | tf_op jit(solution)/shard_map/pallas_call | solution.py:348
  27.3 17.0 %shard_map.69 = (f32[1024,128]{1,0:T(8,128)}, f32[1,64]{1,0:T(1,128)}) custom-call(f32[1024,128]{1,0:T(8,128)} %get-tuple-element.6.hess_ref, f32[1,64]{1,0:T(1,128)} %get-tuple-element.7.grad_ref), custom_call_target="tpu_custom_call" | custom-call | tf_op jit(solution)/shard_map/pallas_call | solution.py:379

commit v3 on v2

--- a/solution.py
+++ b/solution.py
@@ -329,14 +329,20 @@
         gram_copy(mine, step).wait_send()
 
 
-def hand_over(hess_ref, grad_ref, hess_out, grad_out, sem):
-    copies = (
-        pltpu.make_async_copy(hess_ref, hess_out, sem.at[0]),
-        pltpu.make_async_copy(grad_ref, grad_out, sem.at[1]),
-    )
-    for copy in copies:
+def hand_over(hess_ref, grad_ref, hess_out, grad_out, hess, grad, in_sem, out_sem):
+    pieces = 8
+    height = hess.shape[0] // pieces
+    steps = [(hess_ref.at[pl.ds(i * height, height)], hess.at[pl.ds(i * height, height)],
+              hess_out.at[pl.ds(i * height, height)]) for i in range(pieces)]
+    steps.append((grad_ref, grad, grad_out))
+    arriving = [pltpu.make_async_copy(s[0], s[1], in_sem.at[i]) for i, s in enumerate(steps)]
+    leaving = [pltpu.make_async_copy(s[1], s[2], out_sem.at[i]) for i, s in enumerate(steps)]
+    for copy in arriving:
         copy.start()
-    for copy in copies:
+    for one, other in zip(arriving, leaving):
+        one.wait()
+        other.start()
+    for copy in leaving:
         copy.wait()
 
 
@@ -384,7 +390,12 @@
         ),
         in_specs=[pl.BlockSpec(memory_space=pltpu.HBM)] * 2,
         out_specs=[pl.BlockSpec(memory_space=pltpu.HBM)] * 2,
-        scratch_shapes=[pltpu.SemaphoreType.DMA((2,))],
+        scratch_shapes=[
+            pltpu.VMEM((share, 128), jnp.float32),
+            pltpu.VMEM((1, 64), jnp.float32),
+            pltpu.SemaphoreType.DMA((9,)),
+            pltpu.SemaphoreType.DMA((9,)),
+        ],
         compiler_params=pltpu.CompilerParams(vmem_limit_bytes=60 * 2**20),
     )(hessian, gradient)
     return hessian, gradient.reshape(64)

time: 44.5 us -> 29.4 us (0.66)
  Pallas kernels: 43.7 us -> 28.5 us
    pallas_call x1, Pallas kernels: 17 us -> 1.85 us  [gathered(): pl.pallas_call(hand_over, out_shape=(jax.ShapeDtypeStruct((share, 128), j...]
where the time goes in v3:
time: 29.4 us; the launch traced here: 29.2 us
  Pallas kernels  28.5 us (97%)
  between operations  0.64 us (2%)
    pallas_call x1, Pallas kernels, gathered(): pl.pallas_call(functools.partial(kernel, sizes), out_shape=(jax.ShapeDtyp...  26.7 us
    pallas_call x1, Pallas kernels, gathered(): pl.pallas_call(hand_over, out_shape=(jax.ShapeDtypeStruct((share, 128), j...  1.85 us

profile of v3, /device:TPU:29, one launch (start us, length us, event | category | flops | bytes accessed | tf_op | source)
XLA Modules:
  0.0 29.2 jit_solution(11224276660215522646)
XLA Ops:
  0.6 26.7 %shard_map.68 = (f32[1024,128]{1,0:T(8,128)}, f32[1,64]{1,0:T(1,128)}) custom-call(bf16[3,2,8,128]{3,2,1,0:T(8,128)(2,1)} %coef_hbm.1, f32[2,8,128]{2,1,0:T(8,128)} %sigma_hbm.1, f32[2,8,128]{2,1,0:T(8,128)} %resid_hbm.1, s32[1,8]{1,0:T(1,128)} %bitcast.6, bf16[3,16,1024]{2,1,0:T(8,128)(2,1)} %bitcast.5), custom_call_target="tpu_custom_call" | custom-call | tf_op jit(solution)/shard_map/pallas_call | solution.py:354
  27.3 1.9 %shard_map.69 = (f32[1024,128]{1,0:T(8,128)}, f32[1,64]{1,0:T(1,128)}) custom-call(f32[1024,128]{1,0:T(8,128)} %get-tuple-element.6.hess_ref, f32[1,64]{1,0:T(1,128)} %get-tuple-element.7.grad_ref), custom_call_target="tpu_custom_call" | custom-call | tf_op jit(solution)/shard_map/pallas_call | solution.py:385
